TPU v7x, 32 devices: a whole 2x2x4 slice. The times are simulated.
32 devices in a mesh: lat: 8 (over z, x), rad: 4 (over y, core).
Axes of the slice: x: 2, y: 2, z: 4, core: 2. Of those that a mesh axis runs over, the one named last changes fastest.
Arguments:
- kernels: float32 [3, 256000], P(None, 'lat'), may hold values from -6 to 6
- cells: int32 [3, 2048], P(None, 'lat'), may hold values from 0 to 251, as said below
- tiles: int32 [2048, 1], P('lat'), may hold values from 0 to 7; in each aligned block of 256 rows (0 to 255, 256 to 511, ...) at most 64 rows name the same one
- width_class: int32 [8], P('lat'), may hold values from 0 to 3
Outputs:
- smoothed: float32 [3, 64, 128, 256], P(None, 'lat', 'rad')
Inputs may be any that keep to these rules, and one draw needn't show every extreme that they name: `tiles`: of the elements of one index of lat, at most 64 name the same tile, a bound that some block reaches of them. cells[0, e] <= 3, cells[1, e] <= 123 and cells[2, e] <= 251, so that each element's 5 x 5 x 5 block lies in its tile; each bound is reached.
All inputs are finite; a program needn't handle non-finite values.
Results may differ from a plain program's by a relative error of at most 0.000078.
Values sent between devices are 32-bit elements; how exact they have to be, the bound alone decides.
A program may use at most 192 MiB of HBM per device.

v0:
```python
import jax
import jax.numpy as jnp
from jax import lax
from jax.sharding import PartitionSpec as P

CX = 8
NY = 256
CZ = 32
NGLL = 125
HW = 4
HY = 8
HZ = 4


def padded_2(value, sides, width):
    for axis, dim in sides:
        size, length = (lax.axis_size(axis), value.shape[dim])
        up = [(i, (i + 1) % size) for i in range(size - 1)]
        down = [(j, i) for i, j in up]
        last = lax.slice_in_dim(value, length - width, length, axis=dim)
        first = lax.slice_in_dim(value, 0, width, axis=dim)
        before = lax.ppermute(last, axis, up)
        after = lax.ppermute(first, axis, down)
        value = jnp.concatenate([before, value, after], axis=dim)
    return value


def band_weights(place, count, sigma, half):
    offsets = jnp.arange(-half, half + 1)
    target = place[:, None] + offsets[None, :]
    valid = (target >= 0) & (target < count)
    gauss = jnp.exp(-offsets[None, :].astype(jnp.float32) ** 2 / (2.0 * sigma[:, None] ** 2))
    gauss = jnp.where(valid, gauss, jnp.float32(0.0))
    return gauss / jnp.sum(gauss, axis=1, keepdims=True)


def point_cells(cells, depth):
    points = jnp.arange(NGLL, dtype=jnp.int32)
    along_x = points // 25
    along_z = points // 5 % 5
    along_y = points % 5
    return (
        (cells[0][:, None] + along_x[None, :]) * (depth * NY)
        + (cells[1][:, None] + along_z[None, :]) * NY
        + (cells[2][:, None] + along_y[None, :])
    )


def on_device(kernels, cells, tiles, width_class):
    n_lat = lax.axis_size("lat")
    n_rad = lax.axis_size("rad")
    elements = tiles.shape[0]
    capacity = max(2, 2 * elements // n_lat)
    depth = CZ * n_rad
    rows_total = CX * n_lat
    onehot = (tiles == jnp.arange(n_lat)[None, :]).astype(jnp.int32)
    ranks = jnp.cumsum(onehot, axis=0) - onehot
    slot_rank = jnp.sum(ranks * onehot, axis=1)
    slot_index = tiles[:, 0] * capacity + slot_rank
    send_vals = (
        jnp.zeros((3, n_lat * capacity, NGLL), jnp.float32)
        .at[:, slot_index]
        .set(kernels.reshape(3, elements, NGLL))
    )
    recv_vals = lax.all_to_all(
        send_vals.reshape(3, n_lat, capacity * NGLL), "lat", split_axis=1, concat_axis=1, tiled=True
    )
    recv_vals = recv_vals.reshape(3, -1)
    flat_cells = point_cells(cells, depth)
    send_cells = jnp.full((n_lat * capacity, NGLL), -1, jnp.int32).at[slot_index].set(flat_cells)
    recv_cells = lax.all_to_all(
        send_cells.reshape(n_lat, capacity * NGLL), "lat", split_axis=0, concat_axis=0, tiled=True
    )
    recv_cells = recv_cells.reshape(-1)
    slab = lax.axis_index("rad")
    cell_x = recv_cells // (depth * NY)
    cell_z = recv_cells // NY % depth - slab * CZ
    cell_y = recv_cells % NY
    inside = (recv_cells >= 0) & (cell_z >= 0) & (cell_z < CZ)
    local_cell = jnp.where(inside, (cell_x * CZ + cell_z) * NY + cell_y, CX * CZ * NY)
    summed = jnp.zeros((3, CX * CZ * NY), jnp.float32).at[:, local_cell].add(recv_vals, mode="drop")
    summed = summed.reshape(3, CX, CZ, NY)
    tile_index = lax.axis_index("lat")
    rows_here = tile_index * CX + jnp.arange(CX)
    sigma_x = jnp.full((CX,), 1.0, jnp.float32) + 0.75 * width_class[0].astype(jnp.float32)
    weights_x = band_weights(rows_here, rows_total, sigma_x, HW)
    padded = padded_2(summed, (("lat", 1),), HW)
    lateral = jnp.zeros_like(summed)
    for offset in range(-HW, HW + 1):
        lateral = (
            lateral
            + weights_x[:, offset + HW][None, :, None, None]
            * padded[:, HW + offset : HW + offset + CX]
        )
    every_y = jnp.arange(NY)
    weights_y = band_weights(every_y, NY, jnp.full((NY,), 2.5, jnp.float32), HY)
    gaps_y = every_y[None, :] - every_y[:, None]
    matrix_y = jnp.zeros((NY, NY), jnp.float32)
    for offset in range(-HY, HY + 1):
        matrix_y = matrix_y + jnp.where(
            gaps_y == offset, weights_y[:, offset + HY][:, None], jnp.float32(0.0)
        )
    across = jnp.einsum("cxzy,wy->cxzw", lateral, matrix_y, precision=lax.Precision.HIGHEST)
    planes_here = slab * CZ + jnp.arange(CZ)
    weights_z = band_weights(planes_here, depth, jnp.full((CZ,), 1.5, jnp.float32), HZ)
    padded_z = padded_2(across, (("rad", 2),), HZ)
    smoothed = jnp.zeros_like(across)
    for offset in range(-HZ, HZ + 1):
        smoothed = (
            smoothed
            + weights_z[:, offset + HZ][None, None, :, None]
            * padded_z[:, :, HZ + offset : HZ + offset + CZ]
        )
    return smoothed


def solution(mesh):
    return jax.shard_map(
        on_device,
        mesh=mesh,
        in_specs=(P(None, "lat"), P(None, "lat"), P("lat", None), P("lat")),
        out_specs=P(None, "lat", "rad", None),
        check_vma=False,
    )
```

profile of v0, /device:TPU:6, one launch (start us, length us, event | category | flops | bytes accessed | tf_op | source)
XLA Modules:
  0.0 476.4 jit_solution(710803126705207065)
XLA Ops:
  0.0 0.7 fusion.196
  0.7 0.6 reduce-window.6
  1.3 0.2 slice_reduce_fusion
  1.5 0.8 fusion.195
  2.3 0.7 compare_select_fusion.3
  3.0 0.8 fusion.222
  3.8 1.4 scatter_custom_fusion
  5.2 1.2 all_to_all.9
  6.4 6.3 %all-to-all-start = ((s32[8,1,8000]{2,1,0:T(1,128)}), s32[8,1,8000]{2,1,0:T(1,128)S(1)}, u32[]{:S(2)}, u32[]{:S(2)}) async-start(s32[8,1,8000]{2,1,0:T(1,128)} %all_to_all.9), calls=%async_computation | async-start | bytes 516096 | tf_op jit(solution)/shard_map/all_to_all | solution.py:71
  12.8 1.8 reshape.360
  14.6 0.3 copy.39
  14.9 0.1 broadcast_in_dim.194
  15.0 7.0 %scatter_fusion = f32[3,512,125]{2,0,1:T(4,128)S(1)} fusion(f32[3,512,125]{2,0,1:T(4,128)S(1)} %broadcast_in_dim.194, s32[256]{0:T(256)S(1)} %bitcast.89, f32[256,3,125]{2,1,0:T(4,128)S(1)} %bitcast.81), kind=kCustom, calls=%fused_computation.1 | custom fusion | bytes 1153024 | tf_op jit(solution)/shard_map/scatter | solution.py:63
  22.0 0.1 copy.28
  22.1 0.5 reshape.346
  22.5 1.3 copy.29
  24.5 0.1 select_reduce_fusion.1
  24.6 0.1 select_reduce_fusion.2
  24.7 0.1 select_divide_fusion.1
  24.7 0.1 select_divide_fusion.2
  24.8 0.0 all-to-all-done
  24.8 6.0 %all-to-all-start.1 = ((f32[3,8,8000]{2,0,1:T(4,128)}), f32[3,8,8000]{2,0,1:T(4,128)S(1)}, u32[]{:S(2)}, u32[]{:S(2)}) async-start(f32[3,8,8000]{2,0,1:T(4,128)} %copy.29), calls=%async_computation.1 | async-start | bytes 2064384 | tf_op jit(solution)/shard_map/all_to_all | solution.py:65
  30.8 0.1 select_reduce_fusion
  30.9 0.1 select_divide_fusion
  31.0 0.6 reduce.1
  31.6 0.3 reshape.344
  31.9 4.7 fusion.136
  36.7 18.4 %all-to-all-done.1 = f32[3,8,8000]{2,0,1:T(4,128)S(1)} async-done(((f32[3,8,8000]{2,0,1:T(4,128)}), f32[3,8,8000]{2,0,1:T(4,128)S(1)}, u32[]{:S(2)}, u32[]{:S(2)}) %all-to-all-start.1) | async-done | bytes 768032 | tf_op jit(solution)/shard_map/all_to_all | solution.py:65
  55.1 0.1 copy.30
  55.1 0.6 reshape.368
  55.7 15.7 %copy.31 = f32[64000,3]{1,0:T(8,128)} copy(f32[64000,3]{0,1:T(4,128)S(1)} %bitcast.80) | data formatting | bytes 1536000 | tf_op jit(solution)/shard_map/reshape | solution.py:68
  71.4 352.5 %scatter_custom_fusion.2 = f32[3,65536]{0,1:T(8,128)} fusion(s32[64000]{0:T(1024)S(1)} %fusion.136, f32[64000,3]{1,0:T(8,128)} %copy.31, f32[]{:T(128)} %constant.133.clone.1), kind=kCustom, calls=%fused_computation.3 | custom fusion | flops 192000 | bytes 786944 | tf_op jit(solution)/shard_map/scatter-add | solution.py:81
  423.9 19.5 %copy.32 = f32[3,8,32,256]{3,2,1,0:T(8,128)S(1)} copy(f32[3,8,32,256]{0,3,2,1:T(8,128)} %bitcast.79) | data formatting | bytes 1572864 | tf_op jit(solution)/shard_map/reshape | solution.py:82
  443.4 0.1 fusion.220
  443.4 2.7 collective-permute-start.1
  446.2 4.2 collective-permute-start
  450.5 5.9 %collective-permute-done.1 = f32[3,4,32,256]{3,2,1,0:T(8,128)S(1)} collective-permute-done((f32[3,4,32,256]{3,2,1,0:T(8,128)S(1)}, f32[3,4,32,256]{3,2,1,0:T(8,128)S(1)}, u32[]{:S(2)}, u32[]{:S(2)}) %collective-permute-start.1) | collective-permute-done | bytes 393248 | tf_op jit(solution)/shard_map/ppermute | solution.py:23
  456.4 8.3 %collective-permute-done = f32[3,4,32,256]{3,2,1,0:T(8,128)S(1)} collective-permute-done((f32[3,4,32,256]{3,2,1,0:T(8,128)S(1)}, f32[3,4,32,256]{3,2,1,0:T(8,128)S(1)}, u32[]{:S(2)}, u32[]{:S(2)}) %collective-permute-start) | collective-permute-done | bytes 393248 | tf_op jit(solution)/shard_map/ppermute | solution.py:22
  464.7 1.8 fusion.26
  466.5 2.0 collective-permute-start.3
  468.6 2.3 collective-permute-start.2
  470.9 0.0 collective-permute-done.3
  470.9 3.6 collective-permute-done.2
  474.5 1.9 fusion.5
  (15 shorter events, 0.2 us)
Async XLA Ops:
  6.4 18.4 %all-to-all-start = ((s32[8,1,8000]{2,1,0:T(1,128)}), s32[8,1,8000]{2,1,0:T(1,128)S(1)}, u32[]{:S(2)}, u32[]{:S(2)}) async-start(s32[8,1,8000]{2,1,0:T(1,128)} %all_to_all.9), calls=%async_computation | async-start | bytes 516096 | tf_op jit(solution)/shard_map/all_to_all | solution.py:71
  24.8 30.3 %all-to-all-start.1 = ((f32[3,8,8000]{2,0,1:T(4,128)}), f32[3,8,8000]{2,0,1:T(4,128)S(1)}, u32[]{:S(2)}, u32[]{:S(2)}) async-start(f32[3,8,8000]{2,0,1:T(4,128)} %copy.29), calls=%async_computation.1 | async-start | bytes 2064384 | tf_op jit(solution)/shard_map/all_to_all | solution.py:65
  443.4 13.0 %collective-permute-start.1 = (f32[3,4,32,256]{3,2,1,0:T(8,128)S(1)}, f32[3,4,32,256]{3,2,1,0:T(8,128)S(1)}, u32[]{:S(2)}, u32[]{:S(2)}) collective-permute-start(f32[3,4,32,256]{3,2,1,0:T(8,128)S(1)} %get-tuple-element.8), channel_id=1, source_target_pairs={{4,0},{8,4},{12,8},{16,12},{20,16},{24,20},{28,24},{5,1},{9,5},{13... | collective-permute-start | bytes 1179656 | tf_op jit(solution)/shard_map/ppermute | solution.py:23
  446.2 18.5 %collective-permute-start = (f32[3,4,32,256]{3,2,1,0:T(8,128)S(1)}, f32[3,4,32,256]{3,2,1,0:T(8,128)S(1)}, u32[]{:S(2)}, u32[]{:S(2)}) collective-permute-start(f32[3,4,32,256]{3,2,1,0:T(8,128)S(1)} %get-tuple-element.7), channel_id=1, source_target_pairs={{0,4},{4,8},{8,12},{12,16},{16,20},{20,24},{24,28},{1,5},{5,9},{9,... | collective-permute-start | bytes 1179656 | tf_op jit(solution)/shard_map/ppermute | solution.py:22
  466.5 4.4 collective-permute-start.3
  468.6 5.9 %collective-permute-start.2 = (f32[3,8,4,256]{3,2,1,0:T(4,128)S(1)}, f32[3,8,4,256]{3,2,1,0:T(4,128)S(1)}, u32[]{:S(2)}, u32[]{:S(2)}) collective-permute-start(f32[3,8,4,256]{3,2,1,0:T(4,128)S(1)} %get-tuple-element.5), channel_id=1, source_target_pairs={{0,1},{1,2},{2,3},{4,5},{5,6},{6,7},{8,9},{9,10},{10,11},{12,13},{... | collective-permute-start | bytes 294920 | tf_op jit(solution)/shard_map/ppermute | solution.py:22
where the time goes:
time: 477 us; the launch traced here: 476 us
  other arithmetic  364 us (76%)
  local copies, waits for them, and re-layouts  49.4 us (10%)
  waiting for transfers between devices  36.3 us (8%)
  starting transfers between devices  23.6 us (5%)
    scatter-add x1, other arithmetic, on_device(): jnp.zeros((3, CX * CZ * NY), jnp.float32).at[:, local_cell]  353 us
    reshape x1, local copies, waits for them, and re-layouts, on_device(): summed = summed.reshape(3, CX, CZ, NY)  19.5 us
    all_to_all x1, waiting for transfers between devices, on_device(): lax.all_to_all(send_vals.reshape(3, n_lat, capacity * NGLL), 'lat', split...  18.4 us
    reshape x2, local copies, waits for them, and re-layouts, on_device(): recv_vals = recv_vals.reshape(3, -1)  16.3 us
    ppermute x2, waiting for transfers between devices, padded_2(): before = lax.ppermute(last, axis, up)  11.9 us
  transfers between devices with their start and end apart: 6, of which 4 were waited for; matrix products, arithmetic and copies ran while one was open for 4% of the time, Pallas kernels for 0%

commit v1 on v0

--- a/solution.py
+++ b/solution.py
@@ -1,3 +1,4 @@
+import functools
 import jax
 import jax.numpy as jnp
 from jax import lax
@@ -10,6 +11,22 @@
 HW = 4
 HY = 8
 HZ = 4
+
+
+def task_bind(local_values, ax_name):
+    state_now = jnp.concatenate(
+        lax.all_to_all(
+            jnp.stack(jnp.split(local_values, lax.axis_size(ax_name), 1), axis=0),
+            ax_name,
+            split_axis=0,
+            concat_axis=0,
+        ),
+        1,
+    )
+    return state_now
+
+
+clear_the_rows = functools.partial(task_bind, ax_name="lat")
 
 
 def padded_2(value, sides, width):
@@ -62,9 +79,7 @@
         .at[:, slot_index]
         .set(kernels.reshape(3, elements, NGLL))
     )
-    recv_vals = lax.all_to_all(
-        send_vals.reshape(3, n_lat, capacity * NGLL), "lat", split_axis=1, concat_axis=1, tiled=True
-    )
+    recv_vals = clear_the_rows(send_vals.reshape(3, n_lat, capacity * NGLL))
     recv_vals = recv_vals.reshape(3, -1)
     flat_cells = point_cells(cells, depth)
     send_cells = jnp.full((n_lat * capacity, NGLL), -1, jnp.int32).at[slot_index].set(flat_cells)

time: 477 us -> 477 us (level)
  waiting for transfers between devices: 36.3 us -> 29.3 us
    reshape x4 -> x2, local copies, waits for them, and re-layouts: 18 us -> 0.52 us  [the longest x1 0.47 us: on_device(): recv_vals = clear_the_rows(send_vals.reshape(3, n_lat, capacity * NGLL))]
    another operation x1 -> x4, local copies, waits for them, and re-layouts: 0.01 us -> 17 us  [the longest x2 16.3 us: on_device(): recv_vals = recv_vals.reshape(3, -1)]
    all_to_all x1, waiting for transfers between devices: 18.4 us -> 12.9 us  [task_bind(): lax.all_to_all(jnp.stack(jnp.split(local_values, lax.axis_size(ax_name),...]
    unnamed x0 -> x7, local copies, waits for them, and re-layouts: none -> 5.03 us
  transfers between devices with their start and end apart: 6 -> 6, of which waited for: 4 -> 4; matrix products, arithmetic and copies ran while one was open for 4% -> 5% of each run, Pallas kernels for 0% -> 0%
where the time goes in v1:
time: 477 us; the launch traced here: 474 us
  other arithmetic  364 us (76%)
  local copies, waits for them, and re-layouts  53.9 us (11%)
  waiting for transfers between devices  29.3 us (6%)
  starting transfers between devices  24 us (5%)
    scatter-add x1, other arithmetic, on_device(): jnp.zeros((3, CX * CZ * NY), jnp.float32).at[:, local_cell]  353 us
    reshape x1, local copies, waits for them, and re-layouts, on_device(): summed = summed.reshape(3, CX, CZ, NY)  19.5 us
    another operation x2, local copies, waits for them, and re-layouts, on_device(): recv_vals = recv_vals.reshape(3, -1)  16.3 us
    ppermute x2, waiting for transfers between devices, padded_2(): before = lax.ppermute(last, axis, up)  14.6 us
    all_to_all x1, waiting for transfers between devices, task_bind(): lax.all_to_all(jnp.stack(jnp.split(local_values, lax.axis_size(ax_name),...  12.9 us
  transfers between devices with their start and end apart: 6, of which 4 were waited for; matrix products, arithmetic and copies ran while one was open for 5% of the time, Pallas kernels for 0%

profile of v1, /device:TPU:6, one launch (start us, length us, event | category | flops | bytes accessed | tf_op | source)
XLA Modules:
  0.0 474.3 jit_solution(15463374406769371708)
XLA Ops:
  0.0 0.7 fusion.204
  0.7 0.6 reduce-window.6
  1.3 0.2 slice_reduce_fusion
  1.5 0.8 fusion.203
  2.3 0.7 compare_select_fusion.3
  3.0 0.8 fusion.230
  3.8 1.4 scatter_custom_fusion
  5.2 1.2 all_to_all.9
  6.4 6.3 %all-to-all-start = ((s32[8,1,8000]{2,1,0:T(1,128)}), s32[8,1,8000]{2,1,0:T(1,128)S(1)}, u32[]{:S(2)}, u32[]{:S(2)}) async-start(s32[8,1,8000]{2,1,0:T(1,128)} %all_to_all.9), calls=%async_computation | async-start | bytes 516096 | tf_op jit(solution)/shard_map/all_to_all | solution.py:86
  12.8 1.8 reshape.360
  14.6 0.3 copy.45
  14.9 0.1 broadcast_in_dim.194
  15.0 7.0 %scatter_fusion = f32[3,512,125]{2,0,1:T(4,128)S(1)} fusion(f32[3,512,125]{2,0,1:T(4,128)S(1)} %broadcast_in_dim.194, s32[256]{0:T(256)S(1)} %bitcast.127, f32[256,3,125]{2,1,0:T(4,128)S(1)} %bitcast.119), kind=kCustom, calls=%fused_computation.1 | custom fusion | bytes 1153024 | tf_op jit(solution)/shard_map/scatter | solution.py:80
  22.0 0.1 copy.35
  22.0 0.5 reshape.346
  22.5 0.7 fusion.190
  23.2 0.7 fusion.189
  23.9 0.7 fusion.188
  24.7 0.7 fusion.187
  25.4 0.7 fusion.186
  26.1 0.7 fusion.185
  26.8 0.7 fusion.184
  27.6 0.7 fusion.183
  29.0 0.1 select_reduce_fusion.1
  29.1 0.1 select_reduce_fusion.2
  29.2 0.1 select_divide_fusion.1
  29.2 0.1 select_divide_fusion.2
  29.3 6.0 %all-to-all-start.1 = ((f32[8,3,1,8000]{3,2,1,0:T(1,128)}), f32[8,3,1,8000]{3,2,1,0:T(1,128)S(1)}, u32[]{:S(2)}, u32[]{:S(2)}) async-start(f32[8,3,1,8000]{3,2,1,0:T(1,128)} %fusion.183), calls=%async_computation.1 | async-start | bytes 1548288 | tf_op jit(solution)/shard_map/all_to_all | solution.py:18
  35.3 0.1 select_reduce_fusion
  35.4 0.1 select_divide_fusion
  35.5 0.6 reduce.1
  36.1 0.3 reshape.344
  36.4 4.7 %fusion.136 = s32[64000]{0:T(1024)S(1)} fusion(s32[64000,1]{0,1:T(1,128)S(1)} %reshape.344, s32[]{:T(128)S(6)} %mul.236), kind=kLoop, calls=%fused_computation.157 | loop fusion | flops 3456000 | bytes 512004 | tf_op jit(solution)/shard_map/select_n | solution.py:96
  41.1 12.9 %all-to-all-done.1 = f32[8,3,1,8000]{3,2,1,0:T(1,128)S(1)} async-done(((f32[8,3,1,8000]{3,2,1,0:T(1,128)}), f32[8,3,1,8000]{3,2,1,0:T(1,128)S(1)}, u32[]{:S(2)}, u32[]{:S(2)}) %all-to-all-start.1) | async-done | bytes 768032 | tf_op jit(solution)/shard_map/all_to_all | solution.py:18
  54.1 0.6 reshape.368
  54.7 15.7 %copy.37 = f32[64000,3]{1,0:T(8,128)} copy(f32[64000,3]{0,1:T(4,128)S(1)} %bitcast.117) | data formatting | bytes 1536000 | tf_op jit(solution)/shard_map/reshape;reshape | solution.py:83
  70.3 352.5 %scatter_custom_fusion.2 = f32[3,65536]{0,1:T(8,128)} fusion(s32[64000]{0:T(1024)S(1)} %fusion.136, f32[64000,3]{1,0:T(8,128)} %copy.37, f32[]{:T(128)} %constant.133.clone.1), kind=kCustom, calls=%fused_computation.3 | custom fusion | flops 192000 | bytes 786944 | tf_op jit(solution)/shard_map/scatter-add | solution.py:96
  422.9 19.5 %copy.38 = f32[3,8,32,256]{3,2,1,0:T(8,128)S(1)} copy(f32[3,8,32,256]{0,3,2,1:T(8,128)} %bitcast.116) | data formatting | bytes 1572864 | tf_op jit(solution)/shard_map/reshape | solution.py:97
  442.3 0.1 fusion.228
  442.4 2.3 collective-permute-start
  444.7 3.7 collective-permute-start.1
  448.5 14.2 %collective-permute-done = f32[3,4,32,256]{3,2,1,0:T(8,128)S(1)} collective-permute-done((f32[3,4,32,256]{3,2,1,0:T(8,128)S(1)}, f32[3,4,32,256]{3,2,1,0:T(8,128)S(1)}, u32[]{:S(2)}, u32[]{:S(2)}) %collective-permute-start) | collective-permute-done | bytes 393248 | tf_op jit(solution)/shard_map/ppermute | solution.py:39
  462.8 1.8 fusion.26
  464.6 1.9 collective-permute-start.2
  466.5 3.6 collective-permute-start.3
  470.2 0.3 collective-permute-done.2
  470.5 1.8 collective-permute-done.3
  472.4 1.9 fusion.5
  (18 shorter events, 0.2 us)
Async XLA Ops:
  6.4 22.9 %all-to-all-start = ((s32[8,1,8000]{2,1,0:T(1,128)}), s32[8,1,8000]{2,1,0:T(1,128)S(1)}, u32[]{:S(2)}, u32[]{:S(2)}) async-start(s32[8,1,8000]{2,1,0:T(1,128)} %all_to_all.9), calls=%async_computation | async-start | bytes 516096 | tf_op jit(solution)/shard_map/all_to_all | solution.py:86
  29.3 24.7 %all-to-all-start.1 = ((f32[8,3,1,8000]{3,2,1,0:T(1,128)}), f32[8,3,1,8000]{3,2,1,0:T(1,128)S(1)}, u32[]{:S(2)}, u32[]{:S(2)}) async-start(f32[8,3,1,8000]{3,2,1,0:T(1,128)} %fusion.183), calls=%async_computation.1 | async-start | bytes 1548288 | tf_op jit(solution)/shard_map/all_to_all | solution.py:18
  442.4 20.4 %collective-permute-start = (f32[3,4,32,256]{3,2,1,0:T(8,128)S(1)}, f32[3,4,32,256]{3,2,1,0:T(8,128)S(1)}, u32[]{:S(2)}, u32[]{:S(2)}) collective-permute-start(f32[3,4,32,256]{3,2,1,0:T(8,128)S(1)} %get-tuple-element.7), channel_id=1, source_target_pairs={{0,4},{4,8},{8,12},{12,16},{16,20},{20,24},{24,28},{1,5},{5,9},{9,... | collective-permute-start | bytes 1179656 | tf_op jit(solution)/shard_map/ppermute | solution.py:39
  444.7 18.0 %collective-permute-start.1 = (f32[3,4,32,256]{3,2,1,0:T(8,128)S(1)}, f32[3,4,32,256]{3,2,1,0:T(8,128)S(1)}, u32[]{:S(2)}, u32[]{:S(2)}) collective-permute-start(f32[3,4,32,256]{3,2,1,0:T(8,128)S(1)} %get-tuple-element.8), channel_id=1, source_target_pairs={{4,0},{8,4},{12,8},{16,12},{20,16},{24,20},{28,24},{5,1},{9,5},{13... | collective-permute-start | bytes 1179656 | tf_op jit(solution)/shard_map/ppermute | solution.py:40
  464.6 5.9 %collective-permute-start.2 = (f32[3,8,4,256]{3,2,1,0:T(4,128)S(1)}, f32[3,8,4,256]{3,2,1,0:T(4,128)S(1)}, u32[]{:S(2)}, u32[]{:S(2)}) collective-permute-start(f32[3,8,4,256]{3,2,1,0:T(4,128)S(1)} %get-tuple-element.5), channel_id=1, source_target_pairs={{0,1},{1,2},{2,3},{4,5},{5,6},{6,7},{8,9},{9,10},{10,11},{12,13},{... | collective-permute-start | bytes 294920 | tf_op jit(solution)/shard_map/ppermute | solution.py:39
  466.5 5.8 %collective-permute-start.3 = (f32[3,8,4,256]{3,2,1,0:T(4,128)S(1)}, f32[3,8,4,256]{3,2,1,0:T(4,128)S(1)}, u32[]{:S(2)}, u32[]{:S(2)}) collective-permute-start(f32[3,8,4,256]{3,2,1,0:T(4,128)S(1)} %get-tuple-element.6), channel_id=1, source_target_pairs={{1,0},{2,1},{3,2},{5,4},{6,5},{7,6},{9,8},{10,9},{11,10},{13,12},{... | collective-permute-start | bytes 294920 | tf_op jit(solution)/shard_map/ppermute | solution.py:40
